TPU v7x, 32 devices: a whole 2x2x4 slice. The times are simulated.
32 devices in a mesh: dom: 8 (over y, x, core), sub: 4 (over z).
Axes of the slice: x: 2, y: 2, z: 4, core: 2. Of those that a mesh axis runs over, the one named last changes fastest.
Arguments:
- adjoint: float32 [3, 128, 96, 128], P(None, 'dom', 'sub'), may hold values from -15 to 15
- base_flow: float32 [3, 128, 96, 128], P(None, 'dom', 'sub'), may hold values from -6 to 6
- stiffness: float32 [128, 96, 128], P('dom', 'sub'), may hold values from 0.5 to 2
- mass_weight: float32 [128, 96, 128], P('dom', 'sub'), may hold values from 0.05 to 0.2
Outputs:
- adjoint_next: float32 [3, 128, 96, 128], P(None, 'dom', 'sub')
All inputs are finite; a program needn't handle non-finite values.
Results may differ from a plain program's by a relative error of at most 0.009.
Values sent between devices are 32-bit elements; how exact they have to be, the bound alone decides.
A program may use at most 64 MiB of HBM per device.

v0:
```python
import jax
import jax.numpy as jnp
import numpy as np
from jax import lax
from jax.sharding import PartitionSpec as P

ITERS = 2


shift_mass = 100.0


def padded_2(cells, sides, width):
    for axis, dim in sides:
        count = lax.axis_size(axis)
        head = lax.slice_in_dim(cells, 0, width, axis=dim)
        tail = lax.slice_in_dim(cells, cells.shape[dim] - width, cells.shape[dim], axis=dim)
        cells = jnp.concatenate(
            [
                lax.ppermute(tail, axis, [(i, (i + 1) % count) for i in range(count)]),
                cells,
                lax.ppermute(head, axis, [((i + 1) % count, i) for i in range(count)]),
            ],
            axis=dim,
        )
    return cells


def legendre_seven(points):
    previous = np.ones(points.shape)
    current = points * 1.0
    for order in range(1, 7):
        following = ((2 * order + 1) * points * current - order * previous) / (order + 1)
        previous = current
        current = following
    return current


def derivative_table():
    degree = 7
    abscissae = np.array(
        [
            -1.0,
            -0.871740148509607,
            -0.591700181433142,
            -0.209299217902479,
            0.209299217902479,
            0.591700181433142,
            0.871740148509607,
            1.0,
        ]
    )
    legendre_values = legendre_seven(abscissae)
    deriv_table = np.zeros((degree + 1, degree + 1))
    for first_index in range(degree + 1):
        for second_index in range(degree + 1):
            if first_index != second_index:
                deriv_table[first_index, second_index] = legendre_values[first_index] / (
                    legendre_values[second_index]
                    * (abscissae[first_index] - abscissae[second_index])
                )
    deriv_table[0, 0] = -degree * (degree + 1) / 4.0
    deriv_table[degree, degree] = degree * (degree + 1) / 4.0
    return deriv_table


def derive(grid_field, blocks, dim_index, transpose):
    matrix = blocks[dim_index].T if transpose else blocks[dim_index]
    if dim_index == 0:
        return jnp.einsum("ij,cjyr->ciyr", matrix, grid_field, precision=lax.Precision.HIGHEST)
    if dim_index == 1:
        return jnp.einsum("ij,cxjr->cxir", matrix, grid_field, precision=lax.Precision.HIGHEST)
    return jnp.einsum("cxyj,ij->cxyi", grid_field, matrix, precision=lax.Precision.HIGHEST)


def seam_pair(length, dim_index, walls):
    position = jnp.arange(length)
    head_mask = position % 8 == 0
    tail_mask = position % 8 == 7
    if walls:
        head_mask = head_mask & (position > 0)
        tail_mask = tail_mask & (position < length - 1)
    view_shape = [1, 1, 1, 1]
    view_shape[dim_index + 1] = length
    return (
        head_mask.astype(jnp.float32).reshape(view_shape),
        tail_mask.astype(jnp.float32).reshape(view_shape),
    )


def wall_mask(length):
    position = jnp.arange(length)
    return ((position > 0) & (position < length - 1)).astype(jnp.float32).reshape((1, 1, 1, length))


def fold_axis(padded, dim_index):
    axis_index = dim_index + 1
    length = padded.shape[axis_index] - 2
    middle_part = lax.slice_in_dim(padded, 1, length + 1, axis=axis_index)
    lower_part = lax.slice_in_dim(padded, 0, length, axis=axis_index)
    upper_part = lax.slice_in_dim(padded, 2, length + 2, axis=axis_index)
    head_mask, tail_mask = seam_pair(length, dim_index, False)
    return middle_part + tail_mask * upper_part + head_mask * lower_part


def assemble(grid_field):
    padded = padded_2(grid_field, (("dom", 1), ("sub", 2)), 1)
    summed = fold_axis(fold_axis(padded, 0), 1)
    head_mask, tail_mask = seam_pair(summed.shape[3], 2, True)
    summed = summed + tail_mask * jnp.roll(summed, -1, 3) + head_mask * jnp.roll(summed, 1, 3)
    return summed * wall_mask(summed.shape[3])


def operate(grid_field, stiffness, mass_weight, blocks):
    element_sum = shift_mass * mass_weight * grid_field
    for dim_index in range(3):
        element_sum = element_sum + derive(
            stiffness * derive(grid_field, blocks, dim_index, False), blocks, dim_index, True
        )
    return assemble(element_sum)


def inner_products(first_field, second_field, weight):
    return jnp.sum(first_field * second_field * weight, axis=(1, 2, 3))


def as_column(values):
    return values.reshape((3, 1, 1, 1))


def on_device(adjoint, base_flow, stiffness, mass_weight):
    deriv_table = derivative_table()
    blocks = [
        jnp.asarray(np.kron(np.eye(extent // 8), deriv_table), jnp.float32)
        for extent in adjoint.shape[1:]
    ]
    stiffness = stiffness[None]
    mass_weight = mass_weight[None]
    advect = jnp.zeros_like(adjoint)
    transport_list = []
    for dim_index in range(3):
        grad_adjoint = derive(adjoint, blocks, dim_index, False)
        advect = advect + base_flow[dim_index][None] * grad_adjoint
        grad_base = derive(base_flow, blocks, dim_index, False)
        transport_list.append(jnp.sum(adjoint * grad_base, axis=0))
    transport = jnp.stack(transport_list)
    right_side = assemble(mass_weight * (shift_mass * adjoint + advect - transport))
    multiple = jnp.ones((1, 1, 1, 1), jnp.float32)
    for dim_index in range(3):
        head_mask, tail_mask = seam_pair(adjoint.shape[dim_index + 1], dim_index, dim_index == 2)
        multiple = multiple * (1.0 + head_mask + tail_mask)
    weight = wall_mask(adjoint.shape[3]) / multiple
    solution = jnp.zeros_like(right_side)
    residual = right_side

    def squares(current):
        return lax.psum(inner_products(current, current, weight), ("dom", "sub"))

    direction = right_side
    norm_now = squares(residual)
    for iteration in range(ITERS):
        operator_image = operate(direction, stiffness, mass_weight, blocks)
        curvature_sum = lax.psum(inner_products(direction, operator_image, weight), ("dom", "sub"))
        step_length = as_column(norm_now / curvature_sum)
        solution = solution + step_length * direction
        residual = residual - step_length * operator_image
        if iteration + 1 < ITERS:
            norm_next = squares(residual)
            direction = residual + as_column(norm_next / norm_now) * direction
            norm_now = norm_next
    return solution


def solution(mesh):
    in_specs = (
        P(None, "dom", "sub", None),
        P(None, "dom", "sub", None),
        P("dom", "sub", None),
        P("dom", "sub", None),
    )
    out_specs = P(None, "dom", "sub", None)
    return jax.shard_map(
        on_device, mesh=mesh, in_specs=in_specs, out_specs=out_specs, check_vma=False
    )
```

profile of v0, /device:TPU:0, one launch (start us, length us, event | category | flops | bytes accessed | tf_op | source)
XLA Modules:
  0.0 175.9 jit_solution(10872586959832526940)
XLA Ops:
  0.0 1.8 %fusion.64 = f32[24,3,16,128]{3,0,2,1:T(8,128)S(1)} fusion(f32[24,24,1,1]{1,0,3,2:T(8,128)} %constant.124, f32[3,16,24,128]{3,2,1,0:T(8,128)} %param.7), kind=kOutput, calls=%fused_computation.137 | convolution fusion | flops 42467328 | bytes 1181952 | tf_op jit(solution)/shard_map/ij,cxjr->cxir/dot_general | solution.py:72
  1.8 0.6 fusion.17
  2.5 0.9 copy-done.4
  3.4 0.7 copy-done.6
  4.1 0.8 fusion.16
  4.9 0.6 fusion.18
  5.8 0.8 fusion.15
  6.5 0.7 fusion.13
  7.3 0.5 collective-permute-start
  7.9 2.9 %collective-permute-start.1 = (f32[3,1,24,128]{3,1,2,0:T(1,128)S(1)}, f32[3,1,24,128]{3,1,2,0:T(1,128)S(1)}, u32[]{:S(2)}, u32[]{:S(2)}) collective-permute-start(f32[3,1,24,128]{3,1,2,0:T(1,128)S(1)} %get-tuple-element.33), channel_id=1, source_target_pairs={{4,0},{8,4},{12,8},{16,12},{20,16},{24,20},{28,24},{0,28},{5,1},{9... | collective-permute-start | bytes 110600 | tf_op jit(solution)/shard_map/ppermute | solution.py:22
  11.0 1.4 collective-permute-done
  12.5 2.3 %collective-permute-start.2 = (f32[3,18,1,128]{3,1,2,0:T(8,128)S(1)}, f32[3,18,1,128]{3,1,2,0:T(8,128)S(1)}, u32[]{:S(2)}, u32[]{:S(2)}) collective-permute-start(f32[3,18,1,128]{3,1,2,0:T(8,128)S(1)} %get-tuple-element.14), channel_id=1, source_target_pairs={{0,1},{1,2},{2,3},{3,0},{4,5},{5,6},{6,7},{7,4},{8,9},{9,10},{10,1... | collective-permute-start | bytes 82952 | tf_op jit(solution)/shard_map/ppermute | solution.py:20
  14.8 2.1 %collective-permute-start.3 = (f32[3,18,1,128]{3,1,2,0:T(8,128)S(1)}, f32[3,18,1,128]{3,1,2,0:T(8,128)S(1)}, u32[]{:S(2)}, u32[]{:S(2)}) collective-permute-start(f32[3,18,1,128]{3,1,2,0:T(8,128)S(1)} %get-tuple-element.15), channel_id=1, source_target_pairs={{1,0},{2,1},{3,2},{0,3},{5,4},{6,5},{7,6},{4,7},{9,8},{10,9},{11,1... | collective-permute-start | bytes 82952 | tf_op jit(solution)/shard_map/ppermute | solution.py:22
  16.9 2.3 %collective-permute-done.2 = f32[3,18,1,128]{3,1,2,0:T(8,128)S(1)} collective-permute-done((f32[3,18,1,128]{3,1,2,0:T(8,128)S(1)}, f32[3,18,1,128]{3,1,2,0:T(8,128)S(1)}, u32[]{:S(2)}, u32[]{:S(2)}) %collective-permute-start.2) | collective-permute-done | bytes 27680 | tf_op jit(solution)/shard_map/ppermute | solution.py:20
  19.2 0.3 collective-permute-done.3
  19.7 0.2 fusion.23
  20.6 0.4 fusion.33
  21.0 0.6 fusion.65
  21.7 0.3 copy-done.2
  21.9 0.8 fusion.3
  22.7 0.7 convolution_multiply_fusion.1
  23.5 0.7 fusion.66
  24.3 0.8 fusion.5
  25.2 0.6 convolution_add_fusion.1
  25.9 2.6 %collective-permute-start.5 = (f32[3,1,24,128]{3,1,2,0:T(1,128)S(1)}, f32[3,1,24,128]{3,1,2,0:T(1,128)S(1)}, u32[]{:S(2)}, u32[]{:S(2)}) collective-permute-start(f32[3,1,24,128]{3,1,2,0:T(1,128)S(1)} %get-tuple-element.27), channel_id=1, source_target_pairs={{4,0},{8,4},{12,8},{16,12},{20,16},{24,20},{28,24},{0,28},{5,1},{9... | collective-permute-start | bytes 110600 | tf_op jit(solution)/shard_map/ppermute | solution.py:22
  28.6 1.6 collective-permute-done.4
  30.2 1.0 collective-permute-start.6
  31.2 2.9 %collective-permute-start.7 = (f32[3,18,1,128]{3,1,2,0:T(8,128)S(1)}, f32[3,18,1,128]{3,1,2,0:T(8,128)S(1)}, u32[]{:S(2)}, u32[]{:S(2)}) collective-permute-start(f32[3,18,1,128]{3,1,2,0:T(8,128)S(1)} %get-tuple-element.13), channel_id=1, source_target_pairs={{1,0},{2,1},{3,2},{0,3},{5,4},{6,5},{7,6},{4,7},{9,8},{10,9},{11,1... | collective-permute-start | bytes 82952 | tf_op jit(solution)/shard_map/ppermute | solution.py:22
  34.2 1.9 %collective-permute-done.6 = f32[3,18,1,128]{3,1,2,0:T(8,128)S(1)} collective-permute-done((f32[3,18,1,128]{3,1,2,0:T(8,128)S(1)}, f32[3,18,1,128]{3,1,2,0:T(8,128)S(1)}, u32[]{:S(2)}, u32[]{:S(2)}) %collective-permute-start.6) | collective-permute-done | bytes 27680 | tf_op jit(solution)/shard_map/ppermute | solution.py:20
  36.3 0.2 fusion.21
  37.1 0.7 multiply_reduce_fusion.1
  37.8 39.1 %all-reduce = (f32[3]{0:T(128)S(1)}, f32[3]{0:T(128)S(1)}) all-reduce(f32[3]{0:T(128)S(1)} %get-tuple-element.6, f32[3]{0:T(128)S(1)} %get-tuple-element.5), channel_id=1, replica_groups=mesh['dom'=8,'sub'=4] {'dom','sub'}, use_global_device_ids=true, to_apply=%region_4.5 | all-reduce | flops 6 | bytes 48 | tf_op jit(solution)/shard_map/psum | solution.py:157
  76.9 0.3 multiply_reduce_fusion
  77.2 41.6 %psum.30 = f32[3]{0:T(128)S(1)} all-reduce(f32[3]{0:T(128)S(1)} %multiply_reduce_fusion), channel_id=1, replica_groups=mesh['dom'=8,'sub'=4] {'dom','sub'}, use_global_device_ids=true, to_apply=%region_8.9 | all-reduce | flops 3 | bytes 24 | tf_op jit(solution)/shard_map/psum | solution.py:157
  118.9 0.7 convolution_multiply_fusion
  119.6 0.8 fusion
  120.4 0.6 fusion.67
  121.1 0.7 fusion.68
  121.9 0.8 fusion.2
  122.8 0.6 convolution_add_fusion
  123.5 2.6 %collective-permute-start.9 = (f32[3,1,24,128]{3,1,2,0:T(1,128)S(1)}, f32[3,1,24,128]{3,1,2,0:T(1,128)S(1)}, u32[]{:S(2)}, u32[]{:S(2)}) collective-permute-start(f32[3,1,24,128]{3,1,2,0:T(1,128)S(1)} %get-tuple-element.21), channel_id=1, source_target_pairs={{4,0},{8,4},{12,8},{16,12},{20,16},{24,20},{28,24},{0,28},{5,1},{9... | collective-permute-start | bytes 110600 | tf_op jit(solution)/shard_map/ppermute | solution.py:22
  126.1 1.6 collective-permute-done.8
  127.9 3.8 %collective-permute-start.11 = (f32[3,18,1,128]{3,1,2,0:T(8,128)S(1)}, f32[3,18,1,128]{3,1,2,0:T(8,128)S(1)}, u32[]{:S(2)}, u32[]{:S(2)}) collective-permute-start(f32[3,18,1,128]{3,1,2,0:T(8,128)S(1)} %get-tuple-element.11), channel_id=1, source_target_pairs={{1,0},{2,1},{3,2},{0,3},{5,4},{6,5},{7,6},{4,7},{9,8},{10,9},{11,1... | collective-permute-start | bytes 82952 | tf_op jit(solution)/shard_map/ppermute | solution.py:22
  131.7 1.9 %collective-permute-done.10 = f32[3,18,1,128]{3,1,2,0:T(8,128)S(1)} collective-permute-done((f32[3,18,1,128]{3,1,2,0:T(8,128)S(1)}, f32[3,18,1,128]{3,1,2,0:T(8,128)S(1)}, u32[]{:S(2)}, u32[]{:S(2)}) %collective-permute-start.10) | collective-permute-done | bytes 27680 | tf_op jit(solution)/shard_map/ppermute | solution.py:20
  133.8 0.2 fusion.19
  134.6 0.6 fusion.42
  135.3 39.5 %psum.31 = f32[3]{0:T(128)S(1)} all-reduce(f32[3]{0:T(128)S(1)} %fusion.42), channel_id=1, replica_groups=mesh['dom'=8,'sub'=4] {'dom','sub'}, use_global_device_ids=true, to_apply=%region_10.11 | all-reduce | flops 3 | bytes 24 | tf_op jit(solution)/shard_map/psum | solution.py:163
  174.9 1.0 copy.53
  (61 shorter events, 4.1 us)
Async XLA Ops:
  0.0 1.8 %copy-start.5 = (f32[24,24,1,1]{1,0,3,2:T(8,128)S(1)}, f32[24,24,1,1]{1,0,3,2:T(8,128)}, u32[]{:S(2)}) copy-start(f32[24,24,1,1]{1,0,3,2:T(8,128)} %constant.124) | copy-start | bytes 6916
  0.0 1.8 %copy-start = (f32[3,16,24,128]{3,2,1,0:T(8,128)S(1)}, f32[3,16,24,128]{3,2,1,0:T(8,128)}, u32[]{:S(2)}) copy-start(f32[3,16,24,128]{3,2,1,0:T(8,128)} %param.7) | copy-start | bytes 1769476
  0.0 1.8 %copy-start.1 = (f32[3,16,24,128]{3,2,1,0:T(8,128)S(1)}, f32[3,16,24,128]{3,2,1,0:T(8,128)}, u32[]{:S(2)}) copy-start(f32[3,16,24,128]{3,2,1,0:T(8,128)} %param.8) | copy-start | bytes 1769476
  2.4 0.9 copy-start.4
  3.4 0.7 copy-start.6
  4.1 0.8 copy-start.3
  7.3 5.0 %collective-permute-start = (f32[3,1,24,128]{3,1,2,0:T(1,128)S(1)}, f32[3,1,24,128]{3,1,2,0:T(1,128)S(1)}, u32[]{:S(2)}, u32[]{:S(2)}) collective-permute-start(f32[3,1,24,128]{3,1,2,0:T(1,128)S(1)} %get-tuple-element.32), channel_id=1, source_target_pairs={{0,4},{4,8},{8,12},{12,16},{16,20},{20,24},{24,28},{28,0},{1,5},{5... | collective-permute-start | bytes 110600 | tf_op jit(solution)/shard_map/ppermute | solution.py:20
  7.9 4.6 %collective-permute-start.1 = (f32[3,1,24,128]{3,1,2,0:T(1,128)S(1)}, f32[3,1,24,128]{3,1,2,0:T(1,128)S(1)}, u32[]{:S(2)}, u32[]{:S(2)}) collective-permute-start(f32[3,1,24,128]{3,1,2,0:T(1,128)S(1)} %get-tuple-element.33), channel_id=1, source_target_pairs={{4,0},{8,4},{12,8},{16,12},{20,16},{24,20},{28,24},{0,28},{5,1},{9... | collective-permute-start | bytes 110600 | tf_op jit(solution)/shard_map/ppermute | solution.py:22
  12.5 6.8 %collective-permute-start.2 = (f32[3,18,1,128]{3,1,2,0:T(8,128)S(1)}, f32[3,18,1,128]{3,1,2,0:T(8,128)S(1)}, u32[]{:S(2)}, u32[]{:S(2)}) collective-permute-start(f32[3,18,1,128]{3,1,2,0:T(8,128)S(1)} %get-tuple-element.14), channel_id=1, source_target_pairs={{0,1},{1,2},{2,3},{3,0},{4,5},{5,6},{6,7},{7,4},{8,9},{9,10},{10,1... | collective-permute-start | bytes 82952 | tf_op jit(solution)/shard_map/ppermute | solution.py:20
  14.8 4.7 %collective-permute-start.3 = (f32[3,18,1,128]{3,1,2,0:T(8,128)S(1)}, f32[3,18,1,128]{3,1,2,0:T(8,128)S(1)}, u32[]{:S(2)}, u32[]{:S(2)}) collective-permute-start(f32[3,18,1,128]{3,1,2,0:T(8,128)S(1)} %get-tuple-element.15), channel_id=1, source_target_pairs={{1,0},{2,1},{3,2},{0,3},{5,4},{6,5},{7,6},{4,7},{9,8},{10,9},{11,1... | collective-permute-start | bytes 82952 | tf_op jit(solution)/shard_map/ppermute | solution.py:22
  21.0 0.9 copy-start.2
  25.9 4.3 %collective-permute-start.4 = (f32[3,1,24,128]{3,1,2,0:T(1,128)S(1)}, f32[3,1,24,128]{3,1,2,0:T(1,128)S(1)}, u32[]{:S(2)}, u32[]{:S(2)}) collective-permute-start(f32[3,1,24,128]{3,1,2,0:T(1,128)S(1)} %get-tuple-element.26), channel_id=1, source_target_pairs={{0,4},{4,8},{8,12},{12,16},{16,20},{20,24},{24,28},{28,0},{1,5},{5... | collective-permute-start | bytes 110600 | tf_op jit(solution)/shard_map/ppermute | solution.py:20
  25.9 4.3 %collective-permute-start.5 = (f32[3,1,24,128]{3,1,2,0:T(1,128)S(1)}, f32[3,1,24,128]{3,1,2,0:T(1,128)S(1)}, u32[]{:S(2)}, u32[]{:S(2)}) collective-permute-start(f32[3,1,24,128]{3,1,2,0:T(1,128)S(1)} %get-tuple-element.27), channel_id=1, source_target_pairs={{4,0},{8,4},{12,8},{16,12},{20,16},{24,20},{28,24},{0,28},{5,1},{9... | collective-permute-start | bytes 110600 | tf_op jit(solution)/shard_map/ppermute | solution.py:22
  30.2 5.9 %collective-permute-start.6 = (f32[3,18,1,128]{3,1,2,0:T(8,128)S(1)}, f32[3,18,1,128]{3,1,2,0:T(8,128)S(1)}, u32[]{:S(2)}, u32[]{:S(2)}) collective-permute-start(f32[3,18,1,128]{3,1,2,0:T(8,128)S(1)} %get-tuple-element.12), channel_id=1, source_target_pairs={{0,1},{1,2},{2,3},{3,0},{4,5},{5,6},{6,7},{7,4},{8,9},{9,10},{10,1... | collective-permute-start | bytes 82952 | tf_op jit(solution)/shard_map/ppermute | solution.py:20
  31.2 4.9 %collective-permute-start.7 = (f32[3,18,1,128]{3,1,2,0:T(8,128)S(1)}, f32[3,18,1,128]{3,1,2,0:T(8,128)S(1)}, u32[]{:S(2)}, u32[]{:S(2)}) collective-permute-start(f32[3,18,1,128]{3,1,2,0:T(8,128)S(1)} %get-tuple-element.13), channel_id=1, source_target_pairs={{1,0},{2,1},{3,2},{0,3},{5,4},{6,5},{7,6},{4,7},{9,8},{10,9},{11,1... | collective-permute-start | bytes 82952 | tf_op jit(solution)/shard_map/ppermute | solution.py:22
  123.4 4.3 %collective-permute-start.8 = (f32[3,1,24,128]{3,1,2,0:T(1,128)S(1)}, f32[3,1,24,128]{3,1,2,0:T(1,128)S(1)}, u32[]{:S(2)}, u32[]{:S(2)}) collective-permute-start(f32[3,1,24,128]{3,1,2,0:T(1,128)S(1)} %get-tuple-element.20), channel_id=1, source_target_pairs={{0,4},{4,8},{8,12},{12,16},{16,20},{20,24},{24,28},{28,0},{1,5},{5... | collective-permute-start | bytes 110600 | tf_op jit(solution)/shard_map/ppermute | solution.py:20
  123.5 4.3 %collective-permute-start.9 = (f32[3,1,24,128]{3,1,2,0:T(1,128)S(1)}, f32[3,1,24,128]{3,1,2,0:T(1,128)S(1)}, u32[]{:S(2)}, u32[]{:S(2)}) collective-permute-start(f32[3,1,24,128]{3,1,2,0:T(1,128)S(1)} %get-tuple-element.21), channel_id=1, source_target_pairs={{4,0},{8,4},{12,8},{16,12},{20,16},{24,20},{28,24},{0,28},{5,1},{9... | collective-permute-start | bytes 110600 | tf_op jit(solution)/shard_map/ppermute | solution.py:22
  127.8 5.8 %collective-permute-start.10 = (f32[3,18,1,128]{3,1,2,0:T(8,128)S(1)}, f32[3,18,1,128]{3,1,2,0:T(8,128)S(1)}, u32[]{:S(2)}, u32[]{:S(2)}) collective-permute-start(f32[3,18,1,128]{3,1,2,0:T(8,128)S(1)} %get-tuple-element.10), channel_id=1, source_target_pairs={{0,1},{1,2},{2,3},{3,0},{4,5},{5,6},{6,7},{7,4},{8,9},{9,10},{10,1... | collective-permute-start | bytes 82952 | tf_op jit(solution)/shard_map/ppermute | solution.py:20
  127.9 5.7 %collective-permute-start.11 = (f32[3,18,1,128]{3,1,2,0:T(8,128)S(1)}, f32[3,18,1,128]{3,1,2,0:T(8,128)S(1)}, u32[]{:S(2)}, u32[]{:S(2)}) collective-permute-start(f32[3,18,1,128]{3,1,2,0:T(8,128)S(1)} %get-tuple-element.11), channel_id=1, source_target_pairs={{1,0},{2,1},{3,2},{0,3},{5,4},{6,5},{7,6},{4,7},{9,8},{10,9},{11,1... | collective-permute-start | bytes 82952 | tf_op jit(solution)/shard_map/ppermute | solution.py:22
where the time goes:
time: 177 us; the launch traced here: 176 us
  blocking collectives  120 us (68%)
  starting transfers between devices  21 us (12%)
  matrix products  13.7 us (8%)
  waiting for transfers between devices  11.2 us (6%)
  other arithmetic  4.73 us (3%)
  local copies, waits for them, and re-layouts  4.69 us (3%)
    psum x2, blocking collectives, squares(): return lax.psum(inner_products(current, current, weight), ('dom', 'sub'))  80.6 us
    psum x1, blocking collectives, on_device(): lax.psum(inner_products(direction, operator_image, weight), ('dom', 'sub'))  39.5 us
    ppermute x6, starting transfers between devices, padded_2(): lax.ppermute(head, axis, [((i + 1) % count, i) for i in range(count)])  17 us
    ppermute x6, waiting for transfers between devices, padded_2(): lax.ppermute(tail, axis, [(i, (i + 1) % count) for i in range(count)])  10.8 us
    dot_general x6, matrix products, derive(): jnp.einsum('ij,cxjr->cxir', matrix, grid_field, precision=lax.Precision.H...  5.3 us
    dot_general x6, matrix products, derive(): jnp.einsum('ij,cjyr->ciyr', matrix, grid_field, precision=lax.Precision.H...  4.39 us
    dot_general x6, matrix products, derive(): jnp.einsum('cxyj,ij->cxyi', grid_field, matrix, precision=lax.Precision.H...  4.04 us
    ppermute x6, starting transfers between devices, padded_2(): lax.ppermute(tail, axis, [(i, (i + 1) % count) for i in range(count)])  4.03 us
  transfers between devices with their start and end apart: 12, of which 8 were waited for; matrix products, arithmetic and copies ran while one was open for 0% of the time, Pallas kernels for 0%

commit v1 on v0

v1 whole, which is shorter than its diff:
```python
import functools

import jax
import jax.numpy as jnp
import ml_dtypes
import numpy as np
from jax import lax
from jax.experimental import pallas as pl
from jax.experimental.pallas import tpu as pltpu
from jax.sharding import PartitionSpec as P

MESH = pl.DeviceIdType.MESH
shift_mass = 100.0

DIRECTIONS = ((1, 0), (-1, 0), (0, 1), (0, -1), (1, 1), (1, -1), (-1, 1), (-1, -1))


def legendre_seven(points):
    previous = np.ones(points.shape)
    current = points * 1.0
    for order in range(1, 7):
        following = ((2 * order + 1) * points * current - order * previous) / (order + 1)
        previous = current
        current = following
    return current


def derivative_table():
    degree = 7
    abscissae = np.array(
        [
            -1.0,
            -0.871740148509607,
            -0.591700181433142,
            -0.209299217902479,
            0.209299217902479,
            0.591700181433142,
            0.871740148509607,
            1.0,
        ]
    )
    legendre_values = legendre_seven(abscissae)
    deriv_table = np.zeros((degree + 1, degree + 1))
    for first_index in range(degree + 1):
        for second_index in range(degree + 1):
            if first_index != second_index:
                deriv_table[first_index, second_index] = legendre_values[first_index] / (
                    legendre_values[second_index]
                    * (abscissae[first_index] - abscissae[second_index])
                )
    deriv_table[0, 0] = -degree * (degree + 1) / 4.0
    deriv_table[degree, degree] = degree * (degree + 1) / 4.0
    return deriv_table


TABLE = derivative_table()


def apply_table(matrix, values):
    even = [values[j] + values[7 - j] for j in range(4)]
    odd = [values[j] - values[7 - j] for j in range(4)]
    result = [None] * 8
    for i in range(4):
        p = q = None
        for j in range(4):
            a = float((matrix[i, j] + matrix[i, 7 - j]) / 2)
            b = float((matrix[i, j] - matrix[i, 7 - j]) / 2)
            p = a * even[j] if p is None else p + a * even[j]
            q = b * odd[j] if q is None else q + b * odd[j]
        result[i] = q + p
        result[7 - i] = q - p
    return result


def split_weights(matrix):
    wide = matrix.astype(np.float32)
    high = wide.astype(ml_dtypes.bfloat16)
    low = (wide - high.astype(np.float32)).astype(high.dtype)
    return np.block([[high, low], [high, np.zeros_like(low)]])


def times_weights(rows, weights):
    high = rows.astype(jnp.bfloat16)
    low = (rows - high.astype(jnp.float32)).astype(jnp.bfloat16)
    both = jnp.concatenate([high, low], axis=1)
    product = jnp.dot(both, weights, preferred_element_type=jnp.float32)
    half = rows.shape[1]
    return product[:, :half] + product[:, half:]


def fold8(values):
    total = values[0:8]
    for start in range(8, values.shape[0], 8):
        total = total + values[start : start + 8]
    return total


def kernel(
    sizes,
    adjoint_hbm,
    base_hbm,
    stiff_hbm,
    mass_hbm,
    wd_ref,
    wt_ref,
    out_ref,
    adj,
    base,
    stiff,
    mass,
    u0,
    u1,
    bf,
    qf,
    tmp,
    sy,
    sc,
    rx,
    ry,
    rc,
    dots_send,
    dots_recv,
    load_sem,
    send_sem,
    recv_sem,
    dot_send_sem,
    dot_recv_sem,
):
    nd, ns, nx, ny, nr = sizes
    plane = nx * ny
    me_d = lax.axis_index("dom")
    me_s = lax.axis_index("sub")
    ndev = nd * ns

    loads = []
    for k, (src, dst) in enumerate(
        ((adjoint_hbm, adj), (base_hbm, base), (mass_hbm, mass), (stiff_hbm, stiff))
    ):
        copy = pltpu.make_async_copy(src, dst, load_sem.at[k])
        copy.start()
        loads.append(copy)

    def other(offset):
        flat = lax.rem(me_d * ns + me_s + offset, ndev)
        return (lax.div(flat, ns), lax.rem(flat, ns))

    barrier = pltpu.get_barrier_semaphore()

    @pl.loop(1, ndev)
    def _(offset):
        pl.semaphore_signal(barrier, inc=1, device_id=other(offset), device_id_type=MESH)

    lane = lax.broadcasted_iota(jnp.int32, (1, nr), 1)
    inner = (lane > 0) & (lane < nr - 1)
    head = jnp.where((lane % 8 == 0) & inner, 1.0, 0.0)
    tail = jnp.where((lane % 8 == 7) & inner, 1.0, 0.0)
    wall = jnp.where(inner, 1.0, 0.0)
    lane_weight = wall / (1.0 + head + tail)

    def fold_lanes(v):
        v = v + tail * pltpu.roll(v, nr - 1, 1) + head * pltpu.roll(v, 1, 1)
        return v * wall

    def row(c, x):
        return slice(c * plane + x * ny, c * plane + (x + 1) * ny)

    def across(c, y):
        return pl.ds(c * plane + y, nx, stride=ny)

    def neighbour(k):
        dx, dy = DIRECTIONS[k]
        return (lax.rem(me_d + dx + nd, nd), lax.rem(me_s + dy + ns, ns))

    sent = []

    def halo_copies(p, c, u):
        copies = []
        for k, (dx, dy) in enumerate(DIRECTIONS):
            if dy == 0:
                src = u.at[pl.ds(c * plane + ((nx - 1) * ny if dx > 0 else 0), ny)]
                dst = rx.at[p, c, k]
            elif dx == 0:
                src, dst = sy.at[p, c, k - 2], ry.at[p, c, k - 2]
            else:
                src, dst = sc.at[p, c, k - 4], rc.at[p, c, k - 4]
            copies.append(
                pltpu.make_async_remote_copy(
                    src_ref=src,
                    dst_ref=dst,
                    send_sem=send_sem.at[p, c, k],
                    recv_sem=recv_sem.at[p, c, k],
                    device_id=neighbour(k),
                    device_id_type=MESH,
                )
            )
        return copies

    def send(p, c, u):
        for k in (2, 3):
            y = ny - 1 if k == 2 else 0
            buf = sy.at[p, c, k - 2]
            buf[...] = u[across(c, y), :]
            for e in range(8, nx, 8):
                lo = c * plane + (e - 1) * ny + y
                hi = c * plane + e * ny + y
                both = u[lo : lo + 1, :] + u[hi : hi + 1, :]
                buf[e - 1 : e, :] = both
                buf[e : e + 1, :] = both
        for k in range(4, 8):
            dx, dy = DIRECTIONS[k]
            at = c * plane + ((nx - 1) * ny if dx > 0 else 0) + (ny - 1 if dy > 0 else 0)
            sc[p, c, k - 4] = u[at : at + 1, :]
        copies = halo_copies(p, c, u)
        for copy in copies:
            copy.start()
        sent.append(copies)
        return copies

    def assemble(p, c, u, dst, copies):
        for copy in copies:
            copy.wait_recv()
        for x in range(nx):
            if x == 0:
                v = u[row(c, 0), :] + rx[p, c, 0]
            elif x == nx - 1:
                v = u[row(c, x), :] + rx[p, c, 1]
            elif x % 8 == 7:
                v = u[row(c, x), :] + u[row(c, x + 1), :]
            elif x % 8 == 0:
                v = u[row(c, x), :] + u[row(c, x - 1), :]
            else:
                v = u[row(c, x), :]
            dst[row(c, x), :] = v
        for e in range(8, ny, 8):
            both = dst[across(c, e - 1), :] + dst[across(c, e), :]
            dst[across(c, e - 1), :] = both
            dst[across(c, e), :] = both
        dst[across(c, 0), :] = dst[across(c, 0), :] + ry[p, c, 0]
        dst[across(c, ny - 1), :] = dst[across(c, ny - 1), :] + ry[p, c, 1]
        for k in range(4, 8):
            dx, dy = DIRECTIONS[k]
            at = c * plane + (0 if dx > 0 else (nx - 1) * ny) + (0 if dy > 0 else ny - 1)
            dst[at : at + 1, :] = dst[at : at + 1, :] + rc[p, c, k - 4]

    def x_groups(c, ref):
        for xe in range(0, nx, 8):
            yield xe, [ref[row(c, xe + i), :] for i in range(8)]

    def y_groups(c, ref):
        for ye in range(0, ny, 8):
            yield ye, [ref[across(c, ye + j), :] for j in range(8)]

    for copy in loads[:3]:
        copy.wait()
    halos = []
    for c in range(3):
        part = slice(c * plane, (c + 1) * plane)
        for ye in range(0, ny, 8):
            grads = apply_table(TABLE, [adj[across(c, ye + j), :] for j in range(8)])
            terms = [base[across(1, ye + j), :] * grads[j] for j in range(8)]
            if c == 1:
                for d in range(3):
                    grads = apply_table(TABLE, [base[across(d, ye + j), :] for j in range(8)])
                    terms = [
                        terms[j] - adj[across(d, ye + j), :] * grads[j] for j in range(8)
                    ]
            for j in range(8):
                tmp[across(c, ye + j), :] = terms[j]
        radial = base[2 * plane : 3 * plane, :] * times_weights(adj[part, :], wd_ref[...])
        if c == 2:
            for d in range(3):
                some = slice(d * plane, (d + 1) * plane)
                radial = radial - adj[some, :] * times_weights(base[some, :], wd_ref[...])
        for xe in range(0, nx, 8):
            grads = apply_table(TABLE, [adj[row(c, xe + i), :] for i in range(8)])
            terms = [base[row(0, xe + i), :] * grads[i] for i in range(8)]
            if c == 0:
                for d in range(3):
                    grads = apply_table(TABLE, [base[row(d, xe + i), :] for i in range(8)])
                    terms = [terms[i] - adj[row(d, xe + i), :] * grads[i] for i in range(8)]
            for i in range(8):
                x = xe + i
                total = (
                    shift_mass * adj[row(c, x), :]
                    + terms[i]
                    + tmp[row(c, x), :]
                    + radial[x * ny : (x + 1) * ny]
                )
                u0[row(c, x), :] = fold_lanes(mass[row(0, x), :] * total)
        if c == 0:
            pl.semaphore_wait(barrier, ndev - 1)
        halos.append(send(0, c, u0))

    loads[3].wait()
    table_t = TABLE.T

    dots = [[None] * 4 for _ in range(3)]

    def add(c, k, values):
        values = fold8(values)
        dots[c][k] = values if dots[c][k] is None else dots[c][k] + values

    for c in range(3):
        part = slice(c * plane, (c + 1) * plane)
        assemble(0, c, u0, bf, halos[c])
        radial = stiff[...] * times_weights(bf[part, :], wd_ref[...])
        radial = times_weights(radial, wt_ref[...])
        for ye, values in y_groups(c, bf):
            grads = apply_table(TABLE, values)
            terms = apply_table(
                table_t, [stiff[across(0, ye + j), :] * grads[j] for j in range(8)]
            )
            for j in range(8):
                tmp[across(c, ye + j), :] = terms[j]
        for xe, values in x_groups(c, bf):
            grads = apply_table(TABLE, values)
            terms = apply_table(
                table_t, [stiff[row(0, xe + i), :] * grads[i] for i in range(8)]
            )
            for i in range(8):
                x = xe + i
                total = (
                    shift_mass * mass[row(0, x), :] * values[i]
                    + terms[i]
                    + tmp[row(c, x), :]
                    + radial[x * ny : (x + 1) * ny]
                )
                total = fold_lanes(total)
                u1[row(c, x), :] = total
                add(c, 0, values[i] * u0[row(c, x), :])
                add(c, 1, values[i] * total)
        halos[c] = send(1, c, u1)

    for c in range(3):
        part = slice(c * plane, (c + 1) * plane)
        assemble(1, c, u1, qf, halos[c])
        radial = times_weights(qf[part, :], wd_ref[...])
        add(c, 3, stiff[...] * radial * radial)
        for ye, values in y_groups(c, qf):
            grads = apply_table(TABLE, values)
            for j in range(8):
                add(c, 3, stiff[across(0, ye + j), :] * grads[j] * grads[j])
        for xe, values in x_groups(c, qf):
            grads = apply_table(TABLE, values)
            for i in range(8):
                x = xe + i
                add(c, 2, values[i] * u1[row(c, x), :])
                add(
                    c,
                    3,
                    stiff[row(0, x), :] * grads[i] * grads[i]
                    + shift_mass * mass[row(0, x), :] * values[i] * values[i],
                )

    packed = jnp.zeros((1, nr), jnp.float32)
    for c in range(3):
        for k in range(4):
            line = jnp.sum(dots[c][k], axis=0, keepdims=True)
            if k < 3:
                line = line * lane_weight
            packed = jnp.where(lane == 4 * c + k, jnp.sum(line, axis=1, keepdims=True), packed)
    dots_send[0] = packed

    def dot_copy(offset):
        return pltpu.make_async_remote_copy(
            src_ref=dots_send.at[0],
            dst_ref=dots_recv.at[offset - 1],
            send_sem=dot_send_sem,
            recv_sem=dot_recv_sem,
            device_id=other(offset),
            device_id_type=MESH,
        )

    @pl.loop(1, ndev)
    def _(offset):
        dot_copy(offset).start()

    pltpu.make_async_copy(dots_recv, dots_recv, dot_recv_sem).wait()
    total = packed + jnp.sum(dots_recv[...], axis=0)

    for c in range(3):
        bb, bq, qq, qaq = [total[:, 4 * c + k : 4 * c + k + 1] for k in range(4)]
        step0 = bb / bq
        rr1 = step0 * step0 * qq - bb
        more = 1.0 + rr1 / bb
        curve = more * more * bq - 2.0 * more * step0 * qq + step0 * step0 * qaq
        step1 = rr1 / curve
        on_b = jnp.broadcast_to(step0 + step1 * more, (1, nr))
        on_q = jnp.broadcast_to(step1 * step0, (1, nr))
        part = slice(c * plane, (c + 1) * plane)
        out_ref[part, :] = on_b * bf[part, :] - on_q * qf[part, :]

    for copies in sent:
        for copy in copies:
            copy.wait_send()
    pltpu.make_async_copy(dots_recv, dots_recv, dot_send_sem).wait()


def on_device(nd, ns, adjoint, base_flow, stiffness, mass_weight):
    _, nx, ny, nr = adjoint.shape
    rows = nx * ny
    blocks = np.kron(np.eye(nr // 8), TABLE)
    wd = jnp.asarray(split_weights(blocks.T))
    wt = jnp.asarray(split_weights(blocks))
    f32 = jnp.float32
    vmem = pl.BlockSpec(memory_space=pltpu.VMEM)
    hbm = pl.BlockSpec(memory_space=pl.ANY)
    ndev = nd * ns
    out = pl.pallas_call(
        functools.partial(kernel, (nd, ns, nx, ny, nr)),
        out_shape=jax.ShapeDtypeStruct((3 * rows, nr), f32),
        in_specs=[hbm] * 4 + [vmem] * 2,
        out_specs=vmem,
        scratch_shapes=[
            pltpu.VMEM((3 * rows, nr), f32),
            pltpu.VMEM((3 * rows, nr), f32),
            pltpu.VMEM((rows, nr), f32),
            pltpu.VMEM((rows, nr), f32),
            pltpu.VMEM((3 * rows, nr), f32),
            pltpu.VMEM((3 * rows, nr), f32),
            pltpu.VMEM((3 * rows, nr), f32),
            pltpu.VMEM((3 * rows, nr), f32),
            pltpu.VMEM((3 * rows, nr), f32),
            pltpu.VMEM((2, 3, 2, nx, nr), f32),
            pltpu.VMEM((2, 3, 4, 1, nr), f32),
            pltpu.VMEM((2, 3, 2, ny, nr), f32),
            pltpu.VMEM((2, 3, 2, nx, nr), f32),
            pltpu.VMEM((2, 3, 4, 1, nr), f32),
            pltpu.VMEM((1, 1, nr), f32),
            pltpu.VMEM((ndev - 1, 1, nr), f32),
            pltpu.SemaphoreType.DMA((4,)),
            pltpu.SemaphoreType.DMA((2, 3, 8)),
            pltpu.SemaphoreType.DMA((2, 3, 8)),
            pltpu.SemaphoreType.DMA,
            pltpu.SemaphoreType.DMA,
        ],
        compiler_params=pltpu.CompilerParams(
            collective_id=0, has_side_effects=True, vmem_limit_bytes=32 * 1024 * 1024
        ),
    )(
        adjoint.reshape(3 * rows, nr),
        base_flow.reshape(3 * rows, nr),
        stiffness.reshape(rows, nr),
        mass_weight.reshape(rows, nr),
        wd,
        wt,
    )
    return out.reshape(adjoint.shape)


def solution(mesh):
    in_specs = (
        P(None, "dom", "sub", None),
        P(None, "dom", "sub", None),
        P("dom", "sub", None),
        P("dom", "sub", None),
    )
    out_specs = P(None, "dom", "sub", None)
    return jax.shard_map(
        functools.partial(on_device, mesh.shape["dom"], mesh.shape["sub"]),
        mesh=mesh,
        in_specs=in_specs,
        out_specs=out_specs,
        check_vma=False,
    )
```

time: 177 us -> 29.5 us (0.17)
  blocking collectives: 120 us -> 0 us
  Pallas kernels: 0 us -> 22.6 us
  starting transfers between devices: 21 us -> 0 us
  matrix products: 13.7 us -> 0 us
  waiting for transfers between devices: 11.2 us -> 0 us
  other arithmetic: 4.73 us -> 0 us
  local copies, waits for them, and re-layouts: 4.69 us -> 6.6 us
    psum x3 -> x0, blocking collectives: 120 us -> none  [the longest x2 80.6 us: squares(): return lax.psum(inner_products(current, current, weight), ('dom', 'sub'))]
    pallas_call x0 -> x1, Pallas kernels: none -> 22.6 us  [on_device(): pl.pallas_call(functools.partial(kernel, (nd, ns, nx, ny, nr)), out_shape...]
    ppermute x12 -> x0, starting transfers between devices: 21 us -> none  [the longest x6 17 us: padded_2(): lax.ppermute(head, axis, [((i + 1) % count, i) for i in range(count)])]
    dot_general x18 -> x0, matrix products: 13.7 us -> none  [the longest x6 5.3 us: derive(): jnp.einsum('ij,cxjr->cxir', matrix, grid_field, precision=lax.Precision.H...]
    ppermute x12 -> x0, waiting for transfers between devices: 11.2 us -> none  [the longest x6 10.8 us: padded_2(): lax.ppermute(tail, axis, [(i, (i + 1) % count) for i in range(count)])]
    unnamed x15 -> x13, local copies, waits for them, and re-layouts: 1.94 us -> 6.6 us
  transfers between devices with their start and end apart: 12 -> 0, of which waited for: 8 -> 0; matrix products, arithmetic and copies ran while one was open for 0% -> 0% of each run, Pallas kernels for 0% -> 0%
where the time goes in v1:
time: 29.5 us; the launch traced here: 29.2 us
  Pallas kernels  22.6 us (77%)
  local copies, waits for them, and re-layouts  6.6 us (22%)
    pallas_call x1, Pallas kernels, on_device(): pl.pallas_call(functools.partial(kernel, (nd, ns, nx, ny, nr)), out_shape...  22.6 us
    unnamed x13, local copies, waits for them, and re-layouts  6.6 us

profile of v1, /device:TPU:0, one launch (start us, length us, event | category | flops | bytes accessed | tf_op | source)
XLA Modules:
  0.0 29.2 jit_solution(14466563925810433399)
XLA Ops:
  0.0 0.0 copy-start
  0.0 1.1 %copy-done = f32[3,16,24,128]{3,2,1,0:T(8,128)S(1)} copy-done((f32[3,16,24,128]{3,2,1,0:T(8,128)S(1)}, f32[3,16,24,128]{3,2,1,0:T(8,128)}, u32[]{:S(2)}) %copy-start) | copy-done | bytes 589848
  1.1 0.0 copy-start.1
  1.1 1.1 %copy-done.1 = f32[3,16,24,128]{3,2,1,0:T(8,128)S(1)} copy-done((f32[3,16,24,128]{3,2,1,0:T(8,128)S(1)}, f32[3,16,24,128]{3,2,1,0:T(8,128)}, u32[]{:S(2)}) %copy-start.1) | copy-done | bytes 589848
  2.1 0.0 copy-start.2
  2.1 0.9 %copy-done.2 = f32[16,24,128]{2,1,0:T(8,128)S(1)} copy-done((f32[16,24,128]{2,1,0:T(8,128)S(1)}, f32[16,24,128]{2,1,0:T(8,128)}, u32[]{:S(2)}) %copy-start.2) | copy-done | bytes 196632
  3.1 0.0 copy-start.3
  3.1 0.9 %copy-done.3 = f32[16,24,128]{2,1,0:T(8,128)S(1)} copy-done((f32[16,24,128]{2,1,0:T(8,128)S(1)}, f32[16,24,128]{2,1,0:T(8,128)}, u32[]{:S(2)}) %copy-start.3) | copy-done | bytes 196632
  4.0 0.0 copy-start.4
  4.0 0.9 %copy-done.4 = bf16[256,256]{1,0:T(8,128)(2,1)S(1)} copy-done((bf16[256,256]{1,0:T(8,128)(2,1)S(1)}, bf16[256,256]{1,0:T(8,128)(2,1)}, u32[]{:S(2)}) %copy-start.4) | copy-done | bytes 131096
  4.9 0.0 copy-start.5
  4.9 0.9 %copy-done.5 = bf16[256,256]{1,0:T(8,128)(2,1)S(1)} copy-done((bf16[256,256]{1,0:T(8,128)(2,1)S(1)}, bf16[256,256]{1,0:T(8,128)(2,1)}, u32[]{:S(2)}) %copy-start.5) | copy-done | bytes 131096
  5.8 22.6 %shard_map.64 = f32[1152,128]{1,0:T(8,128)S(1)} custom-call(f32[1152,128]{1,0:T(8,128)S(1)} %bitcast.6, f32[1152,128]{1,0:T(8,128)S(1)} %bitcast.7, f32[384,128]{1,0:T(8,128)S(1)} %bitcast.8, f32[384,128]{1,0:T(8,128)S(1)} %bitcast.9, bf16[256,256]{1,0:T(8,128)(2,1)S(1)} %copy-done.5, bf16[256,256]{1,0:T(8,128)(2,1)S(1)} %copy-done.4), custom_call_target="tpu_custom_call" | custom-call | tf_op jit(solution)/shard_map/pallas_call | solution.py:409
  28.4 0.8 %copy.8 = f32[3,16,24,128]{3,2,1,0:T(8,128)} copy(f32[3,16,24,128]{3,2,1,0:T(8,128)S(1)} %bitcast.5) | data formatting | bytes 1179648
Async XLA Ops:
  0.0 1.1 %copy-start = (f32[3,16,24,128]{3,2,1,0:T(8,128)S(1)}, f32[3,16,24,128]{3,2,1,0:T(8,128)}, u32[]{:S(2)}) copy-start(f32[3,16,24,128]{3,2,1,0:T(8,128)} %param.6) | copy-start | bytes 1769476
  1.1 1.1 %copy-start.1 = (f32[3,16,24,128]{3,2,1,0:T(8,128)S(1)}, f32[3,16,24,128]{3,2,1,0:T(8,128)}, u32[]{:S(2)}) copy-start(f32[3,16,24,128]{3,2,1,0:T(8,128)} %param.7) | copy-start | bytes 1769476
  2.1 0.9 %copy-start.2 = (f32[16,24,128]{2,1,0:T(8,128)S(1)}, f32[16,24,128]{2,1,0:T(8,128)}, u32[]{:S(2)}) copy-start(f32[16,24,128]{2,1,0:T(8,128)} %param.8) | copy-start | bytes 589828
  3.1 0.9 %copy-start.3 = (f32[16,24,128]{2,1,0:T(8,128)S(1)}, f32[16,24,128]{2,1,0:T(8,128)}, u32[]{:S(2)}) copy-start(f32[16,24,128]{2,1,0:T(8,128)} %param.9) | copy-start | bytes 589828
  4.0 0.9 %copy-start.4 = (bf16[256,256]{1,0:T(8,128)(2,1)S(1)}, bf16[256,256]{1,0:T(8,128)(2,1)}, u32[]{:S(2)}) copy-start(bf16[256,256]{1,0:T(8,128)(2,1)} %constant.5.clone.wt_ref) | copy-start | bytes 393220
  4.9 0.9 %copy-start.5 = (bf16[256,256]{1,0:T(8,128)(2,1)S(1)}, bf16[256,256]{1,0:T(8,128)(2,1)}, u32[]{:S(2)}) copy-start(bf16[256,256]{1,0:T(8,128)(2,1)} %constant.4.clone.wd_ref) | copy-start | bytes 393220

commit v2 on v1

--- a/solution.py
+++ b/solution.py
@@ -11,6 +11,8 @@
 
 MESH = pl.DeviceIdType.MESH
 shift_mass = 100.0
+GROUPS = ((0, 1), (1, 1), (2, 1))
+VMEM_LIMIT = 63 * 1024 * 1024
 
 DIRECTIONS = ((1, 0), (-1, 0), (0, 1), (0, -1), (1, 1), (1, -1), (-1, 1), (-1, -1))
 
@@ -101,13 +103,15 @@
     base_hbm,
     stiff_hbm,
     mass_hbm,
-    wd_ref,
-    wt_ref,
+    wd_hbm,
+    wt_hbm,
     out_ref,
     adj,
     base,
     stiff,
     mass,
+    wd_ref,
+    wt_ref,
     u0,
     u1,
     bf,
@@ -130,25 +134,47 @@
     plane = nx * ny
     me_d = lax.axis_index("dom")
     me_s = lax.axis_index("sub")
-    ndev = nd * ns
 
     loads = []
     for k, (src, dst) in enumerate(
-        ((adjoint_hbm, adj), (base_hbm, base), (mass_hbm, mass), (stiff_hbm, stiff))
+        (
+            (adjoint_hbm, adj),
+            (base_hbm, base),
+            (mass_hbm, mass),
+            (wd_hbm, wd_ref),
+            (stiff_hbm, stiff),
+            (wt_hbm, wt_ref),
+        )
     ):
         copy = pltpu.make_async_copy(src, dst, load_sem.at[k])
         copy.start()
         loads.append(copy)
 
-    def other(offset):
-        flat = lax.rem(me_d * ns + me_s + offset, ndev)
-        return (lax.div(flat, ns), lax.rem(flat, ns))
+    def flip(at, mask):
+        bit, result = 1, at
+        while bit <= mask:
+            if mask & bit:
+                result = result + bit * (1 - 2 * lax.rem(lax.div(at, bit), 2))
+            bit *= 2
+        return result
+
+    def hops(k):
+        return abs(k % ns) + bin(k // ns // 2).count("1")
+
+    flips_d = [flip(me_d, k) for k in range(nd)]
+    flips_s = [flip(me_s, k) for k in range(ns)]
+    partners = sorted(range(1, nd * ns), key=hops, reverse=True)
+
+    def partner(k):
+        return (flips_d[k // ns], flips_s[k % ns])
 
     barrier = pltpu.get_barrier_semaphore()
 
-    @pl.loop(1, ndev)
-    def _(offset):
-        pl.semaphore_signal(barrier, inc=1, device_id=other(offset), device_id_type=MESH)
+    def greet(device):
+        pl.semaphore_signal(barrier, inc=1, device_id=device, device_id_type=MESH)
+
+    for k in partners:
+        greet(partner(k))
 
     lane = lax.broadcasted_iota(jnp.int32, (1, nr), 1)
     inner = (lane > 0) & (lane < nr - 1)
@@ -173,74 +199,71 @@
 
     sent = []
 
-    def halo_copies(p, c, u):
-        copies = []
-        for k, (dx, dy) in enumerate(DIRECTIONS):
-            if dy == 0:
-                src = u.at[pl.ds(c * plane + ((nx - 1) * ny if dx > 0 else 0), ny)]
-                dst = rx.at[p, c, k]
-            elif dx == 0:
-                src, dst = sy.at[p, c, k - 2], ry.at[p, c, k - 2]
-            else:
-                src, dst = sc.at[p, c, k - 4], rc.at[p, c, k - 4]
-            copies.append(
-                pltpu.make_async_remote_copy(
-                    src_ref=src,
-                    dst_ref=dst,
-                    send_sem=send_sem.at[p, c, k],
-                    recv_sem=recv_sem.at[p, c, k],
-                    device_id=neighbour(k),
-                    device_id_type=MESH,
-                )
-            )
-        return copies
-
     def send(p, c, u):
         for k in (2, 3):
             y = ny - 1 if k == 2 else 0
-            buf = sy.at[p, c, k - 2]
-            buf[...] = u[across(c, y), :]
+            buf = sy.at[p, k - 2, c]
+            buf[...] = u[c, across(0, y), :]
             for e in range(8, nx, 8):
-                lo = c * plane + (e - 1) * ny + y
-                hi = c * plane + e * ny + y
-                both = u[lo : lo + 1, :] + u[hi : hi + 1, :]
+                lo = (e - 1) * ny + y
+                hi = e * ny + y
+                both = u[c, lo : lo + 1, :] + u[c, hi : hi + 1, :]
                 buf[e - 1 : e, :] = both
                 buf[e : e + 1, :] = both
         for k in range(4, 8):
             dx, dy = DIRECTIONS[k]
-            at = c * plane + ((nx - 1) * ny if dx > 0 else 0) + (ny - 1 if dy > 0 else 0)
-            sc[p, c, k - 4] = u[at : at + 1, :]
-        copies = halo_copies(p, c, u)
-        for copy in copies:
-            copy.start()
-        sent.append(copies)
-        return copies
-
-    def assemble(p, c, u, dst, copies):
-        for copy in copies:
-            copy.wait_recv()
+            at = ((nx - 1) * ny if dx > 0 else 0) + (ny - 1 if dy > 0 else 0)
+            sc[p, k - 4, c] = u[c, at : at + 1, :]
+        for g, (first, count) in enumerate(GROUPS):
+            if c != first + count - 1:
+                continue
+            some = pl.ds(first, count)
+            for k in (4, 5, 6, 7, 0, 1, 2, 3):
+                dx, dy = DIRECTIONS[k]
+                if dy == 0:
+                    src = u.at[some, pl.ds((nx - 1) * ny if dx > 0 else 0, ny)]
+                    dst = rx.at[p, k, some]
+                elif dx == 0:
+                    src, dst = sy.at[p, k - 2, some], ry.at[p, k - 2, some]
+                else:
+                    src, dst = sc.at[p, k - 4, some], rc.at[p, k - 4, some]
+                copy = pltpu.make_async_remote_copy(
+                    src_ref=src,
+                    dst_ref=dst,
+                    send_sem=send_sem.at[p, g, k],
+                    recv_sem=recv_sem.at[p, g, k],
+                    device_id=neighbour(k),
+                    device_id_type=MESH,
+                )
+                copy.start()
+                sent.append((p, first, copy))
+
+    def assemble(p, c, u, dst):
+        for phase, first, copy in sent:
+            if phase == p and first == c:
+                copy.wait_recv()
         for x in range(nx):
             if x == 0:
-                v = u[row(c, 0), :] + rx[p, c, 0]
+                v = u[c, row(0, 0), :] + rx[p, 0, c]
             elif x == nx - 1:
-                v = u[row(c, x), :] + rx[p, c, 1]
+                v = u[c, row(0, x), :] + rx[p, 1, c]
             elif x % 8 == 7:
-                v = u[row(c, x), :] + u[row(c, x + 1), :]
+                v = u[c, row(0, x), :] + u[c, row(0, x + 1), :]
             elif x % 8 == 0:
-                v = u[row(c, x), :] + u[row(c, x - 1), :]
+                v = u[c, row(0, x), :] + u[c, row(0, x - 1), :]
             else:
-                v = u[row(c, x), :]
+                v = u[c, row(0, x), :]
             dst[row(c, x), :] = v
         for e in range(8, ny, 8):
             both = dst[across(c, e - 1), :] + dst[across(c, e), :]
             dst[across(c, e - 1), :] = both
             dst[across(c, e), :] = both
-        dst[across(c, 0), :] = dst[across(c, 0), :] + ry[p, c, 0]
-        dst[across(c, ny - 1), :] = dst[across(c, ny - 1), :] + ry[p, c, 1]
+        dst[across(c, 0), :] = dst[across(c, 0), :] + ry[p, 0, c]
+        dst[across(c, ny - 1), :] = dst[across(c, ny - 1), :] + ry[p, 1, c]
         for k in range(4, 8):
             dx, dy = DIRECTIONS[k]
             at = c * plane + (0 if dx > 0 else (nx - 1) * ny) + (0 if dy > 0 else ny - 1)
-            dst[at : at + 1, :] = dst[at : at + 1, :] + rc[p, c, k - 4]
+            dst[at : at + 1, :] = dst[at : at + 1, :] + rc[p, k - 4, c]
 
     def x_groups(c, ref):
         for xe in range(0, nx, 8):
@@ -250,9 +273,8 @@
         for ye in range(0, ny, 8):
             yield ye, [ref[across(c, ye + j), :] for j in range(8)]
 
-    for copy in loads[:3]:
+    for copy in loads[:4]:
         copy.wait()
-    halos = []
     for c in range(3):
         part = slice(c * plane, (c + 1) * plane)
         for ye in range(0, ny, 8):
@@ -286,12 +308,13 @@
                     + tmp[row(c, x), :]
                     + radial[x * ny : (x + 1) * ny]
                 )
-                u0[row(c, x), :] = fold_lanes(mass[row(0, x), :] * total)
+                u0[c, row(0, x), :] = fold_lanes(mass[row(0, x), :] * total)
         if c == 0:
-            pl.semaphore_wait(barrier, ndev - 1)
-        halos.append(send(0, c, u0))
-
-    loads[3].wait()
+            pl.semaphore_wait(barrier, nd * ns - 1)
+        send(0, c, u0)
+
+    for copy in loads[4:]:
+        copy.wait()
     table_t = TABLE.T
 
     dots = [[None] * 4 for _ in range(3)]
@@ -302,7 +325,7 @@
 
     for c in range(3):
         part = slice(c * plane, (c + 1) * plane)
-        assemble(0, c, u0, bf, halos[c])
+        assemble(0, c, u0, bf)
         radial = stiff[...] * times_weights(bf[part, :], wd_ref[...])
         radial = times_weights(radial, wt_ref[...])
         for ye, values in y_groups(c, bf):
@@ -326,14 +349,14 @@
                     + radial[x * ny : (x + 1) * ny]
                 )
                 total = fold_lanes(total)
-                u1[row(c, x), :] = total
-                add(c, 0, values[i] * u0[row(c, x), :])
+                u1[c, row(0, x), :] = total
+                add(c, 0, values[i] * u0[c, row(0, x), :])
                 add(c, 1, values[i] * total)
-        halos[c] = send(1, c, u1)
+        send(1, c, u1)
 
     for c in range(3):
         part = slice(c * plane, (c + 1) * plane)
-        assemble(1, c, u1, qf, halos[c])
+        assemble(1, c, u1, qf)
         radial = times_weights(qf[part, :], wd_ref[...])
         add(c, 3, stiff[...] * radial * radial)
         for ye, values in y_groups(c, qf):
@@ -344,7 +367,7 @@
             grads = apply_table(TABLE, values)
             for i in range(8):
                 x = xe + i
-                add(c, 2, values[i] * u1[row(c, x), :])
+                add(c, 2, values[i] * u1[c, row(0, x), :])
                 add(
                     c,
                     3,
@@ -360,21 +383,15 @@
                 line = line * lane_weight
             packed = jnp.where(lane == 4 * c + k, jnp.sum(line, axis=1, keepdims=True), packed)
     dots_send[0] = packed
-
-    def dot_copy(offset):
-        return pltpu.make_async_remote_copy(
+    for k in partners:
+        pltpu.make_async_remote_copy(
             src_ref=dots_send.at[0],
-            dst_ref=dots_recv.at[offset - 1],
+            dst_ref=dots_recv.at[k - 1],
             send_sem=dot_send_sem,
             recv_sem=dot_recv_sem,
-            device_id=other(offset),
+            device_id=partner(k),
             device_id_type=MESH,
-        )
-
-    @pl.loop(1, ndev)
-    def _(offset):
-        dot_copy(offset).start()
-
+        ).start()
     pltpu.make_async_copy(dots_recv, dots_recv, dot_recv_sem).wait()
     total = packed + jnp.sum(dots_recv[...], axis=0)
 
@@ -390,9 +407,8 @@
         part = slice(c * plane, (c + 1) * plane)
         out_ref[part, :] = on_b * bf[part, :] - on_q * qf[part, :]
 
-    for copies in sent:
-        for copy in copies:
-            copy.wait_send()
+    for _, _, copy in sent:
+        copy.wait_send()
     pltpu.make_async_copy(dots_recv, dots_recv, dot_send_sem).wait()
 
 
@@ -404,38 +420,39 @@
     wt = jnp.asarray(split_weights(blocks))
     f32 = jnp.float32
     vmem = pl.BlockSpec(memory_space=pltpu.VMEM)
-    hbm = pl.BlockSpec(memory_space=pl.ANY)
-    ndev = nd * ns
+    hbm = pl.BlockSpec(memory_space=pltpu.HBM)
     out = pl.pallas_call(
         functools.partial(kernel, (nd, ns, nx, ny, nr)),
         out_shape=jax.ShapeDtypeStruct((3 * rows, nr), f32),
-        in_specs=[hbm] * 4 + [vmem] * 2,
+        in_specs=[hbm] * 6,
         out_specs=vmem,
         scratch_shapes=[
             pltpu.VMEM((3 * rows, nr), f32),
             pltpu.VMEM((3 * rows, nr), f32),
             pltpu.VMEM((rows, nr), f32),
             pltpu.VMEM((rows, nr), f32),
+            pltpu.VMEM(wd.shape, wd.dtype),
+            pltpu.VMEM(wt.shape, wt.dtype),
+            pltpu.VMEM((3, rows, nr), f32),
+            pltpu.VMEM((3, rows, nr), f32),
             pltpu.VMEM((3 * rows, nr), f32),
             pltpu.VMEM((3 * rows, nr), f32),
             pltpu.VMEM((3 * rows, nr), f32),
-            pltpu.VMEM((3 * rows, nr), f32),
-            pltpu.VMEM((3 * rows, nr), f32),
-            pltpu.VMEM((2, 3, 2, nx, nr), f32),
-            pltpu.VMEM((2, 3, 4, 1, nr), f32),
-            pltpu.VMEM((2, 3, 2, ny, nr), f32),
-            pltpu.VMEM((2, 3, 2, nx, nr), f32),
-            pltpu.VMEM((2, 3, 4, 1, nr), f32),
+            pltpu.VMEM((2, 2, 3, nx, nr), f32),
+            pltpu.VMEM((2, 4, 3, 1, nr), f32),
+            pltpu.VMEM((2, 2, 3, ny, nr), f32),
+            pltpu.VMEM((2, 2, 3, nx, nr), f32),
+            pltpu.VMEM((2, 4, 3, 1, nr), f32),
             pltpu.VMEM((1, 1, nr), f32),
-            pltpu.VMEM((ndev - 1, 1, nr), f32),
-            pltpu.SemaphoreType.DMA((4,)),
-            pltpu.SemaphoreType.DMA((2, 3, 8)),
-            pltpu.SemaphoreType.DMA((2, 3, 8)),
+            pltpu.VMEM((nd * ns - 1, 1, nr), f32),
+            pltpu.SemaphoreType.DMA((6,)),
+            pltpu.SemaphoreType.DMA((2, len(GROUPS), 8)),
+            pltpu.SemaphoreType.DMA((2, len(GROUPS), 8)),
             pltpu.SemaphoreType.DMA,
             pltpu.SemaphoreType.DMA,
         ],
         compiler_params=pltpu.CompilerParams(
-            collective_id=0, has_side_effects=True, vmem_limit_bytes=32 * 1024 * 1024
+            collective_id=0, has_side_effects=True, vmem_limit_bytes=VMEM_LIMIT
         ),
     )(
         adjoint.reshape(3 * rows, nr),

time: 29.5 us -> 24.5 us (0.83)
  local copies, waits for them, and re-layouts: 6.6 us -> 1.92 us
    unnamed x13 -> x1, local copies, waits for them, and re-layouts: 6.6 us -> 1.92 us
where the time goes in v2:
time: 24.5 us; the launch traced here: 24.4 us
  Pallas kernels  22.4 us (91%)
  local copies, waits for them, and re-layouts  1.92 us (8%)
    pallas_call x1, Pallas kernels, on_device(): pl.pallas_call(functools.partial(kernel, (nd, ns, nx, ny, nr)), out_shape...  22.4 us
    unnamed x1, local copies, waits for them, and re-layouts  1.92 us

profile of v2, /device:TPU:0, one launch (start us, length us, event | category | flops | bytes accessed | tf_op | source)
XLA Modules:
  0.0 24.4 jit_solution(5135131370419382539)
XLA Ops:
  0.0 22.4 %shard_map.64 = f32[1152,128]{1,0:T(8,128)} custom-call(f32[1152,128]{1,0:T(8,128)} %bitcast.6, f32[1152,128]{1,0:T(8,128)} %bitcast.7, f32[384,128]{1,0:T(8,128)} %bitcast.8, f32[384,128]{1,0:T(8,128)} %bitcast.9, bf16[256,256]{1,0:T(8,128)(2,1)} %constant.4.clone.wd_hbm, bf16[256,256]{1,0:T(8,128)(2,1)} %constant.5.clone.wt_hbm), custom_call_target="tpu_custom_call" | custom-call | tf_op jit(solution)/shard_map/pallas_call | solution.py:424
  22.4 1.9 %copy.8 = f32[3,16,24,128]{3,2,1,0:T(8,128)} copy(f32[3,16,24,128]{3,2,1,0:T(8,128)} %bitcast.5) | data formatting | bytes 1179648

commit v3 on v2

--- a/solution.py
+++ b/solution.py
@@ -105,7 +105,7 @@
     mass_hbm,
     wd_hbm,
     wt_hbm,
-    out_ref,
+    out_hbm,
     adj,
     base,
     stiff,
@@ -124,7 +124,9 @@
     rc,
     dots_send,
     dots_recv,
+    out_ref,
     load_sem,
+    store_sem,
     send_sem,
     recv_sem,
     dot_send_sem,
@@ -395,6 +397,7 @@
     pltpu.make_async_copy(dots_recv, dots_recv, dot_recv_sem).wait()
     total = packed + jnp.sum(dots_recv[...], axis=0)
 
+    stores = []
     for c in range(3):
         bb, bq, qq, qaq = [total[:, 4 * c + k : 4 * c + k + 1] for k in range(4)]
         step0 = bb / bq
@@ -406,9 +409,16 @@
         on_q = jnp.broadcast_to(step1 * step0, (1, nr))
         part = slice(c * plane, (c + 1) * plane)
         out_ref[part, :] = on_b * bf[part, :] - on_q * qf[part, :]
+        some = pl.ds(c * plane, plane)
+        stores.append(
+            pltpu.make_async_copy(out_ref.at[some], out_hbm.at[some], store_sem.at[c])
+        )
+        stores[-1].start()
 
     for _, _, copy in sent:
         copy.wait_send()
+    for copy in stores:
+        copy.wait()
     pltpu.make_async_copy(dots_recv, dots_recv, dot_send_sem).wait()
 
 
@@ -419,13 +429,12 @@
     wd = jnp.asarray(split_weights(blocks.T))
     wt = jnp.asarray(split_weights(blocks))
     f32 = jnp.float32
-    vmem = pl.BlockSpec(memory_space=pltpu.VMEM)
     hbm = pl.BlockSpec(memory_space=pltpu.HBM)
     out = pl.pallas_call(
         functools.partial(kernel, (nd, ns, nx, ny, nr)),
         out_shape=jax.ShapeDtypeStruct((3 * rows, nr), f32),
         in_specs=[hbm] * 6,
-        out_specs=vmem,
+        out_specs=hbm,
         scratch_shapes=[
             pltpu.VMEM((3 * rows, nr), f32),
             pltpu.VMEM((3 * rows, nr), f32),
@@ -445,7 +454,9 @@
             pltpu.VMEM((2, 4, 3, 1, nr), f32),
             pltpu.VMEM((1, 1, nr), f32),
             pltpu.VMEM((nd * ns - 1, 1, nr), f32),
+            pltpu.VMEM((3 * rows, nr), f32),
             pltpu.SemaphoreType.DMA((6,)),
+            pltpu.SemaphoreType.DMA((3,)),
             pltpu.SemaphoreType.DMA((2, len(GROUPS), 8)),
             pltpu.SemaphoreType.DMA((2, len(GROUPS), 8)),
             pltpu.SemaphoreType.DMA,

time: 24.5 us -> 24.4 us (level)
  no operation moved by 1% of the time
where the time goes in v3:
time: 24.4 us; the launch traced here: 24.2 us
  Pallas kernels  22.3 us (91%)
  local copies, waits for them, and re-layouts  1.92 us (8%)
    pallas_call x1, Pallas kernels, on_device(): pl.pallas_call(functools.partial(kernel, (nd, ns, nx, ny, nr)), out_shape...  22.3 us
    unnamed x1, local copies, waits for them, and re-layouts  1.92 us

profile of v3, /device:TPU:0, one launch (start us, length us, event | category | flops | bytes accessed | tf_op | source)
XLA Modules:
  0.0 24.2 jit_solution(7243710202224322832)
XLA Ops:
  0.0 22.3 %shard_map.64 = f32[1152,128]{1,0:T(8,128)} custom-call(f32[1152,128]{1,0:T(8,128)} %bitcast.6, f32[1152,128]{1,0:T(8,128)} %bitcast.7, f32[384,128]{1,0:T(8,128)} %bitcast.8, f32[384,128]{1,0:T(8,128)} %bitcast.9, bf16[256,256]{1,0:T(8,128)(2,1)} %constant.4.clone.wd_hbm, bf16[256,256]{1,0:T(8,128)(2,1)} %constant.5.clone.wt_hbm), custom_call_target="tpu_custom_call" | custom-call | tf_op jit(solution)/shard_map/pallas_call | solution.py:433
  22.3 1.9 %copy.8 = f32[3,16,24,128]{3,2,1,0:T(8,128)} copy(f32[3,16,24,128]{3,2,1,0:T(8,128)} %bitcast.5) | data formatting | bytes 1179648
